TPU v7x, 512 devices: a whole 4x8x8 slice. The times are simulated.
512 devices in a mesh: blk: 128 (over y, x, z_lo, core), pitch: 4 (over z_hi).
Axes of the slice: x: 4, y: 8, z: 8 (z_hi: 4, z_lo: 2; z = z_hi * 2 + z_lo), core: 2. Of those that a mesh axis runs over, the one named last changes fastest.
Arguments:
- flow_state: float32 [5, 32, 2048, 128], P(None, 'pitch', 'blk'), may hold values from -0.6 to 3.2, as said below
- prior_state: float32 [5, 32, 2048, 128], P(None, 'pitch', 'blk'), may hold values from -0.75 to 3.35, as said below
- fourier_store: float32 [2, 49, 10, 2048, 128], P(None, None, None, ('blk', 'pitch')), may hold values from -0.15 to 2.6, as said below
- sample_times: int32 [2, 2048, 128], P(None, ('blk', 'pitch')), may hold values from 0 to 95
- harmonics: int32 [2048, 128], P(('blk', 'pitch')), may hold values from 12 to 24
Outputs:
- new_state: float32 [5, 32, 2048, 128], P(None, 'pitch', 'blk')
- new_store: float32 [2, 49, 10, 2048, 128], P(None, None, None, ('blk', 'pitch'))
- new_ghosts: float32 [2, 10, 2048, 128], P(None, None, ('blk', 'pitch'))
Inputs may be any that keep to these rules, and one draw needn't show every extreme that they name: `flow_state`: density between 0.7 and 1.3, momenta between -0.6 and 0.6, total energy between 2.2 and 3.2. `prior_state`: each entry within 0.15 of flow_state's. `fourier_store`: the k-th cosine and sine coefficients are at most 0.08 / k in magnitude.
All inputs are finite; a program needn't handle non-finite values.
Results may differ from a plain program's by a relative error of at most 0.000068.
Values sent between devices are 32-bit elements; how exact they have to be, the bound alone decides.
A program may use at most 64 MiB of HBM per device.

v0:
```python
import math
import jax
import jax.numpy as jnp
from jax import lax
from jax.sharding import PartitionSpec as P

NT = 96
gamma_less = 0.4
diss_coeff = 0.03125
section_coefs = (1.0 / 3.0, 0.5, 1.0)
pseudo_step = 0.1
physical_step = 0.25
relax_rate = 0.125
lag_turns = 0.3


def padded_2(block, sides, width):
    for axis, dim in sides:
        count = lax.axis_size(axis)
        forward = [(i, i + 1) for i in range(count - 1)]
        backward = [(target, source) for source, target in forward]
        low = lax.ppermute(
            lax.slice_in_dim(block, block.shape[dim] - width, None, axis=dim), axis, forward
        )
        high = lax.ppermute(lax.slice_in_dim(block, 0, width, axis=dim), axis, backward)
        block = jnp.concatenate([low, block, high], axis=dim)
    return block


def fluxes(current, direction):
    density = current[0]
    velocity = current[direction] / density
    pressure = gamma_less * (
        current[4]
        - 0.5
        * (current[1] * current[1] + current[2] * current[2] + current[3] * current[3])
        / density
    )
    flux_parts = [
        current[direction],
        current[1] * velocity,
        current[2] * velocity,
        current[3] * velocity,
        (current[4] + pressure) * velocity,
    ]
    flux_parts[direction] = flux_parts[direction] + pressure
    return jnp.stack(flux_parts)


def face_sum(padded, direction):
    cells_n = padded.shape[direction] - 4
    faces_n = cells_n + 1
    cell_flux = fluxes(padded, direction)

    def window(values, offset, length):
        return lax.slice_in_dim(values, offset, offset + length, axis=direction)

    face_flux = 0.5 * (
        window(cell_flux, 1, faces_n) + window(cell_flux, 2, faces_n)
    ) - diss_coeff * (
        window(padded, 3, faces_n)
        - 3.0 * window(padded, 2, faces_n)
        + 3.0 * window(padded, 1, faces_n)
        - window(padded, 0, faces_n)
    )
    return window(face_flux, 1, cells_n) - window(face_flux, 0, cells_n)


def harmonic_tables(phases_at, harm_count):
    orders = jnp.arange(1, harm_count + 1).astype(jnp.float32).reshape((harm_count, 1, 1))
    angles = orders * phases_at[None]
    return (jnp.cos(angles), jnp.sin(angles))


def rebuild(coeffs, phases_at, active):
    harm_count = (coeffs.shape[0] - 1) // 2
    cosines, sines = harmonic_tables(phases_at, harm_count)
    orders = jnp.arange(1, harm_count + 1).reshape((harm_count, 1, 1))
    active_mask = (orders <= active[None]).astype(jnp.float32)
    harm_terms = (
        coeffs[1 : harm_count + 1] * (active_mask * cosines)[:, None]
        + coeffs[harm_count + 1 :] * (active_mask * sines)[:, None]
    )
    return coeffs[0] + jnp.sum(harm_terms, axis=0)


def refresh(coeffs, samples, phases_at):
    harm_count = (coeffs.shape[0] - 1) // 2
    cosines, sines = harmonic_tables(phases_at, harm_count)
    mean_part = (1.0 - relax_rate) * coeffs[0] + relax_rate * samples
    cos_part = (1.0 - relax_rate) * coeffs[1 : harm_count + 1] + 2.0 * relax_rate * samples[
        None
    ] * cosines[:, None]
    sin_part = (1.0 - relax_rate) * coeffs[harm_count + 1 :] + 2.0 * relax_rate * samples[
        None
    ] * sines[:, None]
    return jnp.concatenate([mean_part[None], cos_part, sin_part], axis=0)


def shards(flow_state, prior_state, fourier_store, sample_times, harmonics):
    pitch_at = lax.axis_index("pitch")
    pitch_end = lax.axis_size("pitch") - 1
    blk_at = lax.axis_index("blk")
    blk_end = lax.axis_size("blk") - 1
    block_rows = flow_state.shape[2]
    radial_cells = flow_state.shape[3]
    period = 2.0 * math.pi / NT
    phase_lag = 2.0 * math.pi * lag_turns
    phases = sample_times.astype(jnp.float32) * period
    low_share = rebuild(fourier_store[0], phases[0] - phase_lag, harmonics)
    high_share = rebuild(fourier_store[1], phases[1] + phase_lag, harmonics)
    low_whole, high_whole = (
        lax.all_gather(low_share, "pitch", axis=1, tiled=True),
        lax.all_gather(high_share, "pitch", axis=1, tiled=True),
    )
    ghost_shape = (5, 2, block_rows, radial_cells)
    low_ghost = low_whole.reshape(ghost_shape)
    high_ghost = high_whole.reshape(ghost_shape)
    current = flow_state
    for section_coef in section_coefs:
        padded = padded_2(current, (("blk", 2), ("pitch", 1)), 2)
        pitch_pad = padded[:, :, 2:-2, :]
        axial_pad = padded[:, 2:-2, :, :]
        pitch_pad = jnp.concatenate(
            [
                jnp.where(pitch_at == 0, low_ghost, pitch_pad[:, :2]),
                current,
                jnp.where(pitch_at == pitch_end, high_ghost, pitch_pad[:, -2:]),
            ],
            axis=1,
        )
        lower_edge = jnp.broadcast_to(current[:, :, :1], axial_pad[:, :, :2].shape)
        upper_edge = jnp.broadcast_to(current[:, :, -1:], axial_pad[:, :, :2].shape)
        axial_pad = jnp.concatenate(
            [
                jnp.where(blk_at == 0, lower_edge, axial_pad[:, :, :2]),
                current,
                jnp.where(blk_at == blk_end, upper_edge, axial_pad[:, :, -2:]),
            ],
            axis=2,
        )
        radial_pad = jnp.pad(current, ((0, 0), (0, 0), (0, 0), (2, 2)), mode="edge")
        summed = face_sum(pitch_pad, 1) + face_sum(axial_pad, 2) + face_sum(radial_pad, 3)
        summed = summed + (3.0 * current - 4.0 * flow_state + prior_state) * (0.5 / physical_step)
        current = flow_state - section_coef * pseudo_step * summed
    face_shape = (10, block_rows, radial_cells)
    upper_face = current[:, -2:].reshape(face_shape)
    lower_face = current[:, :2].reshape(face_shape)
    nothing = jnp.zeros_like(lower_face)
    upper_mine, lower_mine = (
        lax.psum_scatter(
            jnp.where(pitch_at == pitch_end, upper_face, nothing),
            "pitch",
            scatter_dimension=1,
            tiled=True,
        ),
        lax.psum_scatter(
            jnp.where(pitch_at == 0, lower_face, nothing), "pitch", scatter_dimension=1, tiled=True
        ),
    )
    next_phases = phases + period
    low_store = refresh(fourier_store[0], upper_mine, next_phases[0])
    high_store = refresh(fourier_store[1], lower_mine, next_phases[1])
    ghosts = jnp.stack(
        [
            rebuild(low_store, next_phases[0] - phase_lag, harmonics),
            rebuild(high_store, next_phases[1] + phase_lag, harmonics),
        ]
    )
    return (current, jnp.stack([low_store, high_store]), ghosts)


def solution(mesh):
    placed = (
        P(None, "pitch", "blk", None),
        P(None, "pitch", "blk", None),
        P(None, None, None, ("blk", "pitch"), None),
        P(None, ("blk", "pitch"), None),
        P(("blk", "pitch"), None),
    )
    return jax.shard_map(
        shards,
        mesh=mesh,
        in_specs=placed,
        out_specs=(
            P(None, "pitch", "blk", None),
            P(None, None, None, ("blk", "pitch"), None),
            P(None, None, ("blk", "pitch"), None),
        ),
        check_vma=False,
    )
```

profile of v0, /device:TPU:2, one launch (start us, length us, event | category | flops | bytes accessed | tf_op | source)
XLA Modules:
  0.0 193.3 jit_solution(2830352598039493379)
XLA Ops:
  7.2 1.8 fusion.120
  9.0 3.7 %collective-permute-start.1 = (f32[5,8,2,128]{3,2,1,0:T(2,128)}, f32[5,8,2,128]{3,2,1,0:T(2,128)S(1)}, u32[]{:S(2)}, u32[]{:S(2)}) collective-permute-start(f32[5,8,2,128]{3,2,1,0:T(2,128)} %get-tuple-element.91), channel_id=1, source_target_pairs={{4,0},{8,4},{12,8},{16,12},{20,16},{24,20},{28,24},{32,28},{36,32}... | collective-permute-start | bytes 122888 | tf_op jit(solution)/shard_map/ppermute | solution.py:25
  12.7 1.9 collective-permute-start
  14.6 1.6 fusion.119
  16.3 1.2 fusion.121
  17.5 0.7 broadcast_add_fusion
  18.2 2.9 %multiply_sine_fusion.3 = (f32[24,4,128]{2,1,0:T(4,128)S(1)}, f32[24,4,128]{2,1,0:T(4,128)S(1)}, f32[24,4,128]{2,1,0:T(4,128)S(1)}, f32[24,4,128]{2,1,0:T(4,128)...) fusion(f32[4,128]{1,0:T(4,128)S(1)} %get-tuple-element.134, ...), kind=kLoop, calls=%fused_computation.261 | loop fusion | flops 184320 | bytes 604352 | tf_op jit(solution)/shard_map/sin | solution.py:72
  21.2 0.4 fusion.49
  21.6 0.6 bitcast_add_fusion
  22.2 0.6 copy.51
  24.3 1.1 fusion.16
  25.4 18.4 %all_gather.6 = f32[10,16,128]{2,0,1:T(8,128)S(1)} all-gather(f32[10,4,128]{2,0,1:T(8,128)S(1)} %copy-done.4), channel_id=1, replica_groups=mesh['blk'=128,'pitch'=4] {'pitch'}, dimensions={1}, use_global_device_ids=true | all-gather | bytes 102400 | tf_op jit(solution)/shard_map/all_gather | solution.py:113
  43.8 0.7 copy.53
  44.6 14.0 %all_gather.7 = f32[10,16,128]{2,0,1:T(8,128)S(1)} all-gather(f32[10,4,128]{2,0,1:T(8,128)S(1)} %copy.53), channel_id=1, replica_groups=mesh['blk'=128,'pitch'=4] {'pitch'}, dimensions={1}, use_global_device_ids=true | all-gather | bytes 102400 | tf_op jit(solution)/shard_map/all_gather | solution.py:114
  58.7 0.8 broadcast_select_fusion.2
  59.4 0.8 broadcast_select_fusion.5
  60.2 0.9 fusion.25
  61.2 1.3 collective-permute-start.3
  62.5 5.5 %collective-permute-start.2 = (f32[5,2,20,128]{3,2,1,0:T(8,128)S(1)}, f32[5,2,20,128]{3,2,1,0:T(8,128)S(1)}, u32[]{:S(2)}, u32[]{:S(2)}) collective-permute-start(f32[5,2,20,128]{3,2,1,0:T(8,128)S(1)} %get-tuple-element.72), channel_id=1, source_target_pairs={{0,1},{1,2},{2,3},{4,5},{5,6},{6,7},{8,9},{9,10},{10,11},{12,13},{... | collective-permute-start | bytes 307208 | tf_op jit(solution)/shard_map/ppermute | solution.py:22
  68.1 0.4 fusion.43
  68.5 1.7 collective-permute-done.3
  70.7 0.7 copy-done.2
  71.6 0.4 slice_reduce_fusion.2
  72.1 1.9 collective-permute-start.5
  74.0 2.4 %collective-permute-start.4 = (f32[5,8,2,128]{3,2,1,0:T(2,128)S(1)}, f32[5,8,2,128]{3,2,1,0:T(2,128)S(1)}, u32[]{:S(2)}, u32[]{:S(2)}) collective-permute-start(f32[5,8,2,128]{3,2,1,0:T(2,128)S(1)} %get-tuple-element.86), channel_id=1, source_target_pairs={{0,4},{4,8},{8,12},{12,16},{16,20},{20,24},{24,28},{28,32},{32,36}... | collective-permute-start | bytes 122888 | tf_op jit(solution)/shard_map/ppermute | solution.py:22
  77.2 1.1 fusion.9
  78.4 1.8 collective-permute-done.4
  80.4 1.3 collective-permute-start.7
  81.7 6.5 %collective-permute-start.6 = (f32[5,2,20,128]{3,2,1,0:T(8,128)S(1)}, f32[5,2,20,128]{3,2,1,0:T(8,128)S(1)}, u32[]{:S(2)}, u32[]{:S(2)}) collective-permute-start(f32[5,2,20,128]{3,2,1,0:T(8,128)S(1)} %get-tuple-element.70), channel_id=1, source_target_pairs={{0,1},{1,2},{2,3},{4,5},{5,6},{6,7},{8,9},{9,10},{10,11},{12,13},{... | collective-permute-start | bytes 307208 | tf_op jit(solution)/shard_map/ppermute | solution.py:22
  88.7 3.4 %collective-permute-done.7 = f32[5,2,20,128]{3,2,1,0:T(8,128)S(1)} collective-permute-done((f32[5,2,20,128]{3,2,1,0:T(8,128)S(1)}, f32[5,2,20,128]{3,2,1,0:T(8,128)S(1)}, u32[]{:S(2)}, u32[]{:S(2)}) %collective-permute-start.7) | collective-permute-done | bytes 102432 | tf_op jit(solution)/shard_map/ppermute | solution.py:25
  92.7 0.4 slice_reduce_fusion
  93.1 3.7 %collective-permute-start.9 = (f32[5,8,2,128]{3,2,1,0:T(2,128)S(1)}, f32[5,8,2,128]{3,2,1,0:T(2,128)S(1)}, u32[]{:S(2)}, u32[]{:S(2)}) collective-permute-start(f32[5,8,2,128]{3,2,1,0:T(2,128)S(1)} %get-tuple-element.79), channel_id=1, source_target_pairs={{4,0},{8,4},{12,8},{16,12},{20,16},{24,20},{28,24},{32,28},{36,32}... | collective-permute-start | bytes 122888 | tf_op jit(solution)/shard_map/ppermute | solution.py:25
  96.8 1.9 collective-permute-start.8
  99.5 1.1 fusion.2
  100.7 2.3 %collective-permute-done.8 = f32[5,8,2,128]{3,2,1,0:T(2,128)S(1)} collective-permute-done((f32[5,8,2,128]{3,2,1,0:T(2,128)S(1)}, f32[5,8,2,128]{3,2,1,0:T(2,128)S(1)}, u32[]{:S(2)}, u32[]{:S(2)}) %collective-permute-start.8) | collective-permute-done | bytes 40992 | tf_op jit(solution)/shard_map/ppermute | solution.py:22
  103.2 1.3 collective-permute-start.11
  104.5 6.2 %collective-permute-start.10 = (f32[5,2,20,128]{3,2,1,0:T(8,128)S(1)}, f32[5,2,20,128]{3,2,1,0:T(8,128)S(1)}, u32[]{:S(2)}, u32[]{:S(2)}) collective-permute-start(f32[5,2,20,128]{3,2,1,0:T(8,128)S(1)} %get-tuple-element.68), channel_id=1, source_target_pairs={{0,1},{1,2},{2,3},{4,5},{5,6},{6,7},{8,9},{9,10},{10,11},{12,13},{... | collective-permute-start | bytes 307208 | tf_op jit(solution)/shard_map/ppermute | solution.py:22
  110.8 0.4 fusion.29
  111.2 2.4 %collective-permute-done.11 = f32[5,2,20,128]{3,2,1,0:T(8,128)S(1)} collective-permute-done((f32[5,2,20,128]{3,2,1,0:T(8,128)S(1)}, f32[5,2,20,128]{3,2,1,0:T(8,128)S(1)}, u32[]{:S(2)}, u32[]{:S(2)}) %collective-permute-start.11) | collective-permute-done | bytes 102432 | tf_op jit(solution)/shard_map/ppermute | solution.py:25
  114.2 0.7 slice_select_fusion.1
  115.0 1.3 dynamic-slice
  116.9 63.3 %all-reduce.5.cloned.1.call-done = (f32[10,16,128]{2,1,0:T(8,128)}, f32[10,16,128]{2,1,0:T(8,128)}) async-done(((f32[10,16,128]{2,1,0:T(8,128)}, f32[10,16,128]{2,1,0:T(8,128)}), (f32[10,16,128]{2,1,0:T(8,128)}, f32[10,16,128]{2,1,0:T(8,128)})) %all-reduce.5.cloned.1.call-update) | async-done | bytes 163856
  180.2 0.8 dynamic-slice_multiply_fusion
  181.0 0.8 dynamic-slice_multiply_fusion.1
  181.8 0.9 add_reduce_fusion.1
  182.7 0.8 add_bitcast_fusion.1
  183.6 0.6 pad_maximum_fusion.31
  184.6 1.8 pad_maximum_fusion
  (109 shorter events, 6.6 us)
Async XLA Ops:
  7.2 14.0 %copy-start.1 = (f32[2,49,10,4,128]{4,3,2,1,0:T(4,128)S(1)}, f32[2,49,10,4,128]{4,3,2,1,0:T(4,128)}, u32[]{:S(2)}) copy-start(f32[2,49,10,4,128]{4,3,2,1,0:T(4,128)} %param.7) | copy-start | bytes 6021124
  7.2 173.0 %all-reduce.5.cloned.1.call-start = ((), (), s32[]{:S(2)}) async-start(), calls=%async_computation | async-start | bytes 327680
  9.0 49.6 %collective-permute-start.1 = (f32[5,8,2,128]{3,2,1,0:T(2,128)}, f32[5,8,2,128]{3,2,1,0:T(2,128)S(1)}, u32[]{:S(2)}, u32[]{:S(2)}) collective-permute-start(f32[5,8,2,128]{3,2,1,0:T(2,128)} %get-tuple-element.91), channel_id=1, source_target_pairs={{4,0},{8,4},{12,8},{16,12},{20,16},{24,20},{28,24},{32,28},{36,32}... | collective-permute-start | bytes 122888 | tf_op jit(solution)/shard_map/ppermute | solution.py:25
  12.7 46.7 %collective-permute-start = (f32[5,8,2,128]{3,2,1,0:T(2,128)}, f32[5,8,2,128]{3,2,1,0:T(2,128)}, u32[]{:S(2)}, u32[]{:S(2)}) collective-permute-start(f32[5,8,2,128]{3,2,1,0:T(2,128)} %get-tuple-element.92), channel_id=1, source_target_pairs={{0,4},{4,8},{8,12},{12,16},{16,20},{20,24},{24,28},{28,32},{32,36}... | collective-permute-start | bytes 122888 | tf_op jit(solution)/shard_map/ppermute | solution.py:22
  21.2 2.6 %copy-start = (f32[5,8,16,128]{3,2,1,0:T(8,128)S(1)}, f32[5,8,16,128]{3,2,1,0:T(8,128)}, u32[]{:S(2)}) copy-start(f32[5,8,16,128]{3,2,1,0:T(8,128)} %param.5) | copy-start | bytes 983044
  24.1 1.2 copy-start.4
  61.2 9.0 %collective-permute-start.3 = (f32[5,2,20,128]{3,2,1,0:T(8,128)S(1)}, f32[5,2,20,128]{3,2,1,0:T(8,128)S(1)}, u32[]{:S(2)}, u32[]{:S(2)}) collective-permute-start(f32[5,2,20,128]{3,2,1,0:T(8,128)S(1)} %get-tuple-element.71), channel_id=1, source_target_pairs={{1,0},{2,1},{3,2},{5,4},{6,5},{7,6},{9,8},{10,9},{11,10},{13,12},{... | collective-permute-start | bytes 307208 | tf_op jit(solution)/shard_map/ppermute | solution.py:25
  62.5 7.9 %collective-permute-start.2 = (f32[5,2,20,128]{3,2,1,0:T(8,128)S(1)}, f32[5,2,20,128]{3,2,1,0:T(8,128)S(1)}, u32[]{:S(2)}, u32[]{:S(2)}) collective-permute-start(f32[5,2,20,128]{3,2,1,0:T(8,128)S(1)} %get-tuple-element.72), channel_id=1, source_target_pairs={{0,1},{1,2},{2,3},{4,5},{5,6},{6,7},{8,9},{9,10},{10,11},{12,13},{... | collective-permute-start | bytes 307208 | tf_op jit(solution)/shard_map/ppermute | solution.py:22
  70.4 1.0 copy-start.2
  72.1 6.3 %collective-permute-start.5 = (f32[5,8,2,128]{3,2,1,0:T(2,128)S(1)}, f32[5,8,2,128]{3,2,1,0:T(2,128)S(1)}, u32[]{:S(2)}, u32[]{:S(2)}) collective-permute-start(f32[5,8,2,128]{3,2,1,0:T(2,128)S(1)} %get-tuple-element.85), channel_id=1, source_target_pairs={{4,0},{8,4},{12,8},{16,12},{20,16},{24,20},{28,24},{32,28},{36,32}... | collective-permute-start | bytes 122888 | tf_op jit(solution)/shard_map/ppermute | solution.py:25
  74.0 6.2 %collective-permute-start.4 = (f32[5,8,2,128]{3,2,1,0:T(2,128)S(1)}, f32[5,8,2,128]{3,2,1,0:T(2,128)S(1)}, u32[]{:S(2)}, u32[]{:S(2)}) collective-permute-start(f32[5,8,2,128]{3,2,1,0:T(2,128)S(1)} %get-tuple-element.86), channel_id=1, source_target_pairs={{0,4},{4,8},{8,12},{12,16},{16,20},{20,24},{24,28},{28,32},{32,36}... | collective-permute-start | bytes 122888 | tf_op jit(solution)/shard_map/ppermute | solution.py:22
  80.4 11.7 %collective-permute-start.7 = (f32[5,2,20,128]{3,2,1,0:T(8,128)S(1)}, f32[5,2,20,128]{3,2,1,0:T(8,128)S(1)}, u32[]{:S(2)}, u32[]{:S(2)}) collective-permute-start(f32[5,2,20,128]{3,2,1,0:T(8,128)S(1)} %get-tuple-element.69), channel_id=1, source_target_pairs={{1,0},{2,1},{3,2},{5,4},{6,5},{7,6},{9,8},{10,9},{11,10},{13,12},{... | collective-permute-start | bytes 307208 | tf_op jit(solution)/shard_map/ppermute | solution.py:25
  81.7 10.4 %collective-permute-start.6 = (f32[5,2,20,128]{3,2,1,0:T(8,128)S(1)}, f32[5,2,20,128]{3,2,1,0:T(8,128)S(1)}, u32[]{:S(2)}, u32[]{:S(2)}) collective-permute-start(f32[5,2,20,128]{3,2,1,0:T(8,128)S(1)} %get-tuple-element.70), channel_id=1, source_target_pairs={{0,1},{1,2},{2,3},{4,5},{5,6},{6,7},{8,9},{9,10},{10,11},{12,13},{... | collective-permute-start | bytes 307208 | tf_op jit(solution)/shard_map/ppermute | solution.py:22
  93.1 7.6 %collective-permute-start.9 = (f32[5,8,2,128]{3,2,1,0:T(2,128)S(1)}, f32[5,8,2,128]{3,2,1,0:T(2,128)S(1)}, u32[]{:S(2)}, u32[]{:S(2)}) collective-permute-start(f32[5,8,2,128]{3,2,1,0:T(2,128)S(1)} %get-tuple-element.79), channel_id=1, source_target_pairs={{4,0},{8,4},{12,8},{16,12},{20,16},{24,20},{28,24},{32,28},{36,32}... | collective-permute-start | bytes 122888 | tf_op jit(solution)/shard_map/ppermute | solution.py:25
  96.8 6.2 %collective-permute-start.8 = (f32[5,8,2,128]{3,2,1,0:T(2,128)S(1)}, f32[5,8,2,128]{3,2,1,0:T(2,128)S(1)}, u32[]{:S(2)}, u32[]{:S(2)}) collective-permute-start(f32[5,8,2,128]{3,2,1,0:T(2,128)S(1)} %get-tuple-element.80), channel_id=1, source_target_pairs={{0,4},{4,8},{8,12},{12,16},{16,20},{20,24},{24,28},{28,32},{32,36}... | collective-permute-start | bytes 122888 | tf_op jit(solution)/shard_map/ppermute | solution.py:22
  103.2 10.4 %collective-permute-start.11 = (f32[5,2,20,128]{3,2,1,0:T(8,128)S(1)}, f32[5,2,20,128]{3,2,1,0:T(8,128)S(1)}, u32[]{:S(2)}, u32[]{:S(2)}) collective-permute-start(f32[5,2,20,128]{3,2,1,0:T(8,128)S(1)} %get-tuple-element.67), channel_id=1, source_target_pairs={{1,0},{2,1},{3,2},{5,4},{6,5},{7,6},{9,8},{10,9},{11,10},{13,12},{... | collective-permute-start | bytes 307208 | tf_op jit(solution)/shard_map/ppermute | solution.py:25
  104.5 9.1 %collective-permute-start.10 = (f32[5,2,20,128]{3,2,1,0:T(8,128)S(1)}, f32[5,2,20,128]{3,2,1,0:T(8,128)S(1)}, u32[]{:S(2)}, u32[]{:S(2)}) collective-permute-start(f32[5,2,20,128]{3,2,1,0:T(8,128)S(1)} %get-tuple-element.68), channel_id=1, source_target_pairs={{0,1},{1,2},{2,3},{4,5},{5,6},{6,7},{8,9},{9,10},{10,11},{12,13},{... | collective-permute-start | bytes 307208 | tf_op jit(solution)/shard_map/ppermute | solution.py:22
  114.2 68.5 %copy-start.3 = (f32[5,8,16,128]{3,2,1,0:T(8,128)}, f32[5,8,16,128]{3,2,1,0:T(8,128)S(1)}, u32[]{:S(2)}) copy-start(f32[5,8,16,128]{3,2,1,0:T(8,128)S(1)} %fusion.89) | copy-start | bytes 983044
Sparse Core Ops, SparseCore 0:
  115.1 65.0 all-reduce.4
where the time goes:
time: 194 us; the launch traced here: 193 us
  waiting for transfers between devices  75.1 us (39%)
  starting transfers between devices  37.6 us (19%)
  blocking collectives  32.5 us (17%)
  other arithmetic  22.2 us (11%)
  between operations  15.5 us (8%)
  local copies, waits for them, and re-layouts  10.5 us (5%)
    unnamed x2, waiting for transfers between devices  63.3 us
    ppermute x6, starting transfers between devices, padded_2(): lax.ppermute(lax.slice_in_dim(block, block.shape[dim] - width, None, axis...  24.4 us
    all_gather x1, blocking collectives, shards(): lax.all_gather(low_share, 'pitch', axis=1, tiled=True)  18.4 us
    all_gather x1, blocking collectives, shards(): lax.all_gather(high_share, 'pitch', axis=1, tiled=True)  14 us
    ppermute x6, starting transfers between devices, padded_2(): lax.ppermute(lax.slice_in_dim(block, 0, width, axis=dim), axis, backward)  13.1 us
    ppermute x6, waiting for transfers between devices, padded_2(): lax.ppermute(lax.slice_in_dim(block, 0, width, axis=dim), axis, backward)  7.49 us
    sub x9, other arithmetic, face_sum(): 0.5 * (window(cell_flux, 1, faces_n) + window(cell_flux, 2, faces_n))  4.7 us
    ppermute x6, waiting for transfers between devices, padded_2(): lax.ppermute(lax.slice_in_dim(block, block.shape[dim] - width, None, axis...  4.27 us
  transfers between devices with their start and end apart: 13, of which 7 were waited for; matrix products, arithmetic and copies ran while one was open for 10% of the time, Pallas kernels for 0%

commit v1 on v0

--- a/solution.py
+++ b/solution.py
@@ -110,7 +110,9 @@
     low_share = rebuild(fourier_store[0], phases[0] - phase_lag, harmonics)
     high_share = rebuild(fourier_store[1], phases[1] + phase_lag, harmonics)
     low_whole, high_whole = (
-        lax.all_gather(low_share, "pitch", axis=1, tiled=True),
+        jnp.concatenate(
+            lax.all_to_all(jnp.stack([low_share] * lax.axis_size("pitch")), "pitch", 0, 0), axis=1
+        ),
         lax.all_gather(high_share, "pitch", axis=1, tiled=True),
     )
     ghost_shape = (5, 2, block_rows, radial_cells)

time: 194 us -> 187 us (0.964)
  blocking collectives: 32.5 us -> 16.2 us
  starting transfers between devices: 37.6 us -> 46.6 us
    all_gather x1 -> x0, blocking collectives: 18.4 us -> none  [shards(): lax.all_gather(low_share, 'pitch', axis=1, tiled=True)]
    all_to_all x0 -> x1, starting transfers between devices: none -> 9.4 us  [shards(): lax.all_to_all(jnp.stack([low_share] * lax.axis_size('pitch')), 'pitch',...]
    all_gather x1, blocking collectives: 14 us -> 16.2 us  [shards(): lax.all_gather(high_share, 'pitch', axis=1, tiled=True)]
    unnamed x2, waiting for transfers between devices: 63.3 us -> 65.3 us
  transfers between devices with their start and end apart: 13 -> 14, of which waited for: 7 -> 7; matrix products, arithmetic and copies ran while one was open for 10% -> 11% of each run, Pallas kernels for 0% -> 0%
where the time goes in v1:
time: 187 us; the launch traced here: 186 us
  waiting for transfers between devices  75.3 us (40%)
  starting transfers between devices  46.6 us (25%)
  other arithmetic  23.4 us (13%)
  blocking collectives  16.2 us (9%)
  between operations  15.6 us (8%)
  local copies, waits for them, and re-layouts  8.77 us (5%)
    unnamed x2, waiting for transfers between devices  65.3 us
    ppermute x6, starting transfers between devices, padded_2(): lax.ppermute(lax.slice_in_dim(block, block.shape[dim] - width, None, axis...  23.9 us
    all_gather x1, blocking collectives, shards(): lax.all_gather(high_share, 'pitch', axis=1, tiled=True)  16.2 us
    ppermute x6, starting transfers between devices, padded_2(): lax.ppermute(lax.slice_in_dim(block, 0, width, axis=dim), axis, backward)  13.3 us
    all_to_all x1, starting transfers between devices, shards(): lax.all_to_all(jnp.stack([low_share] * lax.axis_size('pitch')), 'pitch',...  9.4 us
    ppermute x6, waiting for transfers between devices, padded_2(): lax.ppermute(lax.slice_in_dim(block, 0, width, axis=dim), axis, backward)  5.69 us
    sub x9, other arithmetic, face_sum(): 0.5 * (window(cell_flux, 1, faces_n) + window(cell_flux, 2, faces_n))  4.7 us
    ppermute x6, waiting for transfers between devices, padded_2(): lax.ppermute(lax.slice_in_dim(block, block.shape[dim] - width, None, axis...  4.24 us
  transfers between devices with their start and end apart: 14, of which 7 were waited for; matrix products, arithmetic and copies ran while one was open for 11% of the time, Pallas kernels for 0%

profile of v1, /device:TPU:2, one launch (start us, length us, event | category | flops | bytes accessed | tf_op | source)
XLA Modules:
  0.0 185.8 jit_solution(10420785069679825950)
XLA Ops:
  7.2 1.2 fusion.120
  8.4 3.7 %collective-permute-start.1 = (f32[5,8,2,128]{3,2,1,0:T(2,128)S(1)}, f32[5,8,2,128]{3,2,1,0:T(2,128)S(1)}, u32[]{:S(2)}, u32[]{:S(2)}) collective-permute-start(f32[5,8,2,128]{3,2,1,0:T(2,128)S(1)} %get-tuple-element.91), channel_id=1, source_target_pairs={{4,0},{8,4},{12,8},{16,12},{20,16},{24,20},{28,24},{32,28},{36,32}... | collective-permute-start | bytes 122888 | tf_op jit(solution)/shard_map/ppermute | solution.py:25
  12.1 1.9 %collective-permute-start = (f32[5,8,2,128]{3,2,1,0:T(2,128)S(1)}, f32[5,8,2,128]{3,2,1,0:T(2,128)S(1)}, u32[]{:S(2)}, u32[]{:S(2)}) collective-permute-start(f32[5,8,2,128]{3,2,1,0:T(2,128)S(1)} %get-tuple-element.92), channel_id=1, source_target_pairs={{0,4},{4,8},{8,12},{12,16},{16,20},{20,24},{24,28},{28,32},{32,36}... | collective-permute-start | bytes 122888 | tf_op jit(solution)/shard_map/ppermute | solution.py:22
  14.0 0.7 broadcast_add_fusion
  14.7 3.8 %multiply_sine_fusion.3 = (f32[24,4,128]{2,1,0:T(4,128)S(1)}, f32[24,4,128]{2,1,0:T(4,128)}, f32[24,4,128]{2,1,0:T(4,128)S(1)}, f32[24,4,128]{2,1,0:T(4,128)S(1)...) fusion(f32[4,128]{1,0:T(4,128)S(1)} %get-tuple-element.134, ...), kind=kLoop, calls=%fused_computation.261 | loop fusion | flops 184320 | bytes 604352 | tf_op jit(solution)/shard_map/sin | solution.py:72
  18.5 1.9 %fusion.49 = (f32[10,4,128]{2,1,0:T(4,128)S(1)}, f32[10,4,128]{2,1,0:T(4,128)S(1)}) fusion(f32[2,49,10,4,128]{4,3,2,1,0:T(4,128)} %param.7, f32[24,4,128]{2,1,0:T(4,128)S(1)} %get-tuple-element.126, f32[24,4,128]{2,1,0:T(4,128)S(1)} %get-tuple-element.125, f32[24,4,128]{2,1,0:T(4,128)S(1)} %get-tuple-element.122, f32[24,4,128]{2,1,0:T(4,128)S(1)} %get-tuple-element.121), kind=kLoop, calls=%fused_computation.90 | loop fusion | flops 972800 | bytes 2203648 | tf_op jit(solution)/shard_map/reduce_sum | solution.py:84
  20.5 0.6 stack.32
  21.1 9.4 %all-to-all-start = ((f32[4,10,4,128]{3,2,1,0:T(4,128)}), f32[4,10,4,128]{3,2,1,0:T(4,128)}, u32[]{:S(2)}, u32[]{:S(2)}) async-start(f32[4,10,4,128]{3,2,1,0:T(4,128)} %stack.32), calls=%async_computation | async-start | bytes 163840 | tf_op jit(solution)/shard_map/all_to_all | solution.py:114
  31.6 0.3 pad_maximum_fusion.7
  32.1 1.1 fusion.16
  33.3 16.2 %all_gather.3 = f32[10,16,128]{2,0,1:T(8,128)S(1)} all-gather(f32[10,4,128]{2,0,1:T(8,128)S(1)} %copy.53), channel_id=1, replica_groups=mesh['blk'=128,'pitch'=4] {'pitch'}, dimensions={1}, use_global_device_ids=true | all-gather | bytes 102400 | tf_op jit(solution)/shard_map/all_gather | solution.py:116
  49.4 0.7 copy.54
  50.3 0.7 fusion.114
  51.0 1.3 collective-permute-start.3
  52.3 6.1 %collective-permute-start.2 = (f32[5,2,20,128]{3,2,1,0:T(8,128)}, f32[5,2,20,128]{3,2,1,0:T(8,128)}, u32[]{:S(2)}, u32[]{:S(2)}) collective-permute-start(f32[5,2,20,128]{3,2,1,0:T(8,128)} %get-tuple-element.72), channel_id=1, source_target_pairs={{0,1},{1,2},{2,3},{4,5},{5,6},{6,7},{8,9},{9,10},{10,11},{12,13},{... | collective-permute-start | bytes 307208 | tf_op jit(solution)/shard_map/ppermute | solution.py:22
  58.5 0.4 fusion.43
  58.9 0.9 copy.52
  59.8 1.1 collective-permute-done.3
  60.9 0.9 slice_select_fusion.6
  61.8 0.9 slice_select_fusion.7
  63.1 0.7 copy-done.2
  64.0 0.4 slice_reduce_fusion.2
  64.5 1.9 %collective-permute-start.5 = (f32[5,8,2,128]{3,2,1,0:T(2,128)S(1)}, f32[5,8,2,128]{3,2,1,0:T(2,128)S(1)}, u32[]{:S(2)}, u32[]{:S(2)}) collective-permute-start(f32[5,8,2,128]{3,2,1,0:T(2,128)S(1)} %get-tuple-element.85), channel_id=1, source_target_pairs={{4,0},{8,4},{12,8},{16,12},{20,16},{24,20},{28,24},{32,28},{36,32}... | collective-permute-start | bytes 122888 | tf_op jit(solution)/shard_map/ppermute | solution.py:25
  66.4 2.4 %collective-permute-start.4 = (f32[5,8,2,128]{3,2,1,0:T(2,128)S(1)}, f32[5,8,2,128]{3,2,1,0:T(2,128)S(1)}, u32[]{:S(2)}, u32[]{:S(2)}) collective-permute-start(f32[5,8,2,128]{3,2,1,0:T(2,128)S(1)} %get-tuple-element.86), channel_id=1, source_target_pairs={{0,4},{4,8},{8,12},{12,16},{16,20},{20,24},{24,28},{28,32},{32,36}... | collective-permute-start | bytes 122888 | tf_op jit(solution)/shard_map/ppermute | solution.py:22
  69.6 1.1 fusion.9
  70.8 1.8 collective-permute-done.4
  72.8 1.3 collective-permute-start.7
  74.1 5.5 %collective-permute-start.6 = (f32[5,2,20,128]{3,2,1,0:T(8,128)S(1)}, f32[5,2,20,128]{3,2,1,0:T(8,128)S(1)}, u32[]{:S(2)}, u32[]{:S(2)}) collective-permute-start(f32[5,2,20,128]{3,2,1,0:T(8,128)S(1)} %get-tuple-element.70), channel_id=1, source_target_pairs={{0,1},{1,2},{2,3},{4,5},{5,6},{6,7},{8,9},{9,10},{10,11},{12,13},{... | collective-permute-start | bytes 307208 | tf_op jit(solution)/shard_map/ppermute | solution.py:22
  79.7 0.4 fusion.36
  80.1 3.1 %collective-permute-done.7 = f32[5,2,20,128]{3,2,1,0:T(8,128)S(1)} collective-permute-done((f32[5,2,20,128]{3,2,1,0:T(8,128)S(1)}, f32[5,2,20,128]{3,2,1,0:T(8,128)S(1)}, u32[]{:S(2)}, u32[]{:S(2)}) %collective-permute-start.7) | collective-permute-done | bytes 102432 | tf_op jit(solution)/shard_map/ppermute | solution.py:25
  83.7 0.4 slice_reduce_fusion
  84.2 3.8 %collective-permute-start.9 = (f32[5,8,2,128]{3,2,1,0:T(2,128)S(1)}, f32[5,8,2,128]{3,2,1,0:T(2,128)S(1)}, u32[]{:S(2)}, u32[]{:S(2)}) collective-permute-start(f32[5,8,2,128]{3,2,1,0:T(2,128)S(1)} %get-tuple-element.79), channel_id=1, source_target_pairs={{4,0},{8,4},{12,8},{16,12},{20,16},{24,20},{28,24},{32,28},{36,32}... | collective-permute-start | bytes 122888 | tf_op jit(solution)/shard_map/ppermute | solution.py:25
  87.9 1.9 %collective-permute-start.8 = (f32[5,8,2,128]{3,2,1,0:T(2,128)S(1)}, f32[5,8,2,128]{3,2,1,0:T(2,128)S(1)}, u32[]{:S(2)}, u32[]{:S(2)}) collective-permute-start(f32[5,8,2,128]{3,2,1,0:T(2,128)S(1)} %get-tuple-element.80), channel_id=1, source_target_pairs={{0,4},{4,8},{8,12},{12,16},{16,20},{20,24},{24,28},{28,32},{32,36}... | collective-permute-start | bytes 122888 | tf_op jit(solution)/shard_map/ppermute | solution.py:22
  90.7 1.1 fusion.2
  91.9 2.3 %collective-permute-done.8 = f32[5,8,2,128]{3,2,1,0:T(2,128)S(1)} collective-permute-done((f32[5,8,2,128]{3,2,1,0:T(2,128)S(1)}, f32[5,8,2,128]{3,2,1,0:T(2,128)S(1)}, u32[]{:S(2)}, u32[]{:S(2)}) %collective-permute-start.8) | collective-permute-done | bytes 40992 | tf_op jit(solution)/shard_map/ppermute | solution.py:22
  94.3 1.3 collective-permute-start.11
  95.6 6.1 %collective-permute-start.10 = (f32[5,2,20,128]{3,2,1,0:T(8,128)S(1)}, f32[5,2,20,128]{3,2,1,0:T(8,128)S(1)}, u32[]{:S(2)}, u32[]{:S(2)}) collective-permute-start(f32[5,2,20,128]{3,2,1,0:T(8,128)S(1)} %get-tuple-element.68), channel_id=1, source_target_pairs={{0,1},{1,2},{2,3},{4,5},{5,6},{6,7},{8,9},{9,10},{10,11},{12,13},{... | collective-permute-start | bytes 307208 | tf_op jit(solution)/shard_map/ppermute | solution.py:22
  101.9 0.4 fusion.29
  102.3 1.6 collective-permute-done.11
  104.6 0.7 slice_select_fusion.1
  105.4 1.3 dynamic-slice
  107.3 65.3 %all-reduce.5.cloned.1.call-done = (f32[10,16,128]{2,1,0:T(8,128)}, f32[10,16,128]{2,1,0:T(8,128)}) async-done(((f32[10,16,128]{2,1,0:T(8,128)}, f32[10,16,128]{2,1,0:T(8,128)}), (f32[10,16,128]{2,1,0:T(8,128)}, f32[10,16,128]{2,1,0:T(8,128)})) %all-reduce.5.cloned.1.call-update) | async-done | bytes 163856
  172.6 0.8 dynamic-slice_multiply_fusion
  173.4 0.8 dynamic-slice_multiply_fusion.1
  174.3 0.9 add_reduce_fusion.1
  175.2 0.8 add_bitcast_fusion.1
  176.0 0.6 pad_maximum_fusion.31
  177.1 1.8 pad_maximum_fusion
  (124 shorter events, 6.1 us)
Async XLA Ops:
  7.2 23.3 %copy-start = (f32[5,8,16,128]{3,2,1,0:T(8,128)S(1)}, f32[5,8,16,128]{3,2,1,0:T(8,128)}, u32[]{:S(2)}) copy-start(f32[5,8,16,128]{3,2,1,0:T(8,128)} %param.5) | copy-start | bytes 983044
  7.2 13.3 %copy-start.1 = (f32[2,49,10,4,128]{4,3,2,1,0:T(4,128)S(1)}, f32[2,49,10,4,128]{4,3,2,1,0:T(4,128)}, u32[]{:S(2)}) copy-start(f32[2,49,10,4,128]{4,3,2,1,0:T(4,128)} %param.7) | copy-start | bytes 6021124
  8.4 41.7 %collective-permute-start.1 = (f32[5,8,2,128]{3,2,1,0:T(2,128)S(1)}, f32[5,8,2,128]{3,2,1,0:T(2,128)S(1)}, u32[]{:S(2)}, u32[]{:S(2)}) collective-permute-start(f32[5,8,2,128]{3,2,1,0:T(2,128)S(1)} %get-tuple-element.91), channel_id=1, source_target_pairs={{4,0},{8,4},{12,8},{16,12},{20,16},{24,20},{28,24},{32,28},{36,32}... | collective-permute-start | bytes 122888 | tf_op jit(solution)/shard_map/ppermute | solution.py:25
  12.1 38.1 %collective-permute-start = (f32[5,8,2,128]{3,2,1,0:T(2,128)S(1)}, f32[5,8,2,128]{3,2,1,0:T(2,128)S(1)}, u32[]{:S(2)}, u32[]{:S(2)}) collective-permute-start(f32[5,8,2,128]{3,2,1,0:T(2,128)S(1)} %get-tuple-element.92), channel_id=1, source_target_pairs={{0,4},{4,8},{8,12},{12,16},{16,20},{20,24},{24,28},{28,32},{32,36}... | collective-permute-start | bytes 122888 | tf_op jit(solution)/shard_map/ppermute | solution.py:22
  21.1 37.8 %all-to-all-start = ((f32[4,10,4,128]{3,2,1,0:T(4,128)}), f32[4,10,4,128]{3,2,1,0:T(4,128)}, u32[]{:S(2)}, u32[]{:S(2)}) async-start(f32[4,10,4,128]{3,2,1,0:T(4,128)} %stack.32), calls=%async_computation | async-start | bytes 163840 | tf_op jit(solution)/shard_map/all_to_all | solution.py:114
  30.5 142.1 %all-reduce.5.cloned.1.call-start = ((), (), s32[]{:S(2)}) async-start(), calls=%async_computation.1 | async-start | bytes 327680
  51.0 9.9 %collective-permute-start.3 = (f32[5,2,20,128]{3,2,1,0:T(8,128)}, f32[5,2,20,128]{3,2,1,0:T(8,128)}, u32[]{:S(2)}, u32[]{:S(2)}) collective-permute-start(f32[5,2,20,128]{3,2,1,0:T(8,128)} %get-tuple-element.71), channel_id=1, source_target_pairs={{1,0},{2,1},{3,2},{5,4},{6,5},{7,6},{9,8},{10,9},{11,10},{13,12},{... | collective-permute-start | bytes 307208 | tf_op jit(solution)/shard_map/ppermute | solution.py:25
  52.3 9.5 %collective-permute-start.2 = (f32[5,2,20,128]{3,2,1,0:T(8,128)}, f32[5,2,20,128]{3,2,1,0:T(8,128)}, u32[]{:S(2)}, u32[]{:S(2)}) collective-permute-start(f32[5,2,20,128]{3,2,1,0:T(8,128)} %get-tuple-element.72), channel_id=1, source_target_pairs={{0,1},{1,2},{2,3},{4,5},{5,6},{6,7},{8,9},{9,10},{10,11},{12,13},{... | collective-permute-start | bytes 307208 | tf_op jit(solution)/shard_map/ppermute | solution.py:22
  62.8 1.0 copy-start.2
  64.5 6.3 %collective-permute-start.5 = (f32[5,8,2,128]{3,2,1,0:T(2,128)S(1)}, f32[5,8,2,128]{3,2,1,0:T(2,128)S(1)}, u32[]{:S(2)}, u32[]{:S(2)}) collective-permute-start(f32[5,8,2,128]{3,2,1,0:T(2,128)S(1)} %get-tuple-element.85), channel_id=1, source_target_pairs={{4,0},{8,4},{12,8},{16,12},{20,16},{24,20},{28,24},{32,28},{36,32}... | collective-permute-start | bytes 122888 | tf_op jit(solution)/shard_map/ppermute | solution.py:25
  66.4 6.2 %collective-permute-start.4 = (f32[5,8,2,128]{3,2,1,0:T(2,128)S(1)}, f32[5,8,2,128]{3,2,1,0:T(2,128)S(1)}, u32[]{:S(2)}, u32[]{:S(2)}) collective-permute-start(f32[5,8,2,128]{3,2,1,0:T(2,128)S(1)} %get-tuple-element.86), channel_id=1, source_target_pairs={{0,4},{4,8},{8,12},{12,16},{16,20},{20,24},{24,28},{28,32},{32,36}... | collective-permute-start | bytes 122888 | tf_op jit(solution)/shard_map/ppermute | solution.py:22
  72.8 10.3 %collective-permute-start.7 = (f32[5,2,20,128]{3,2,1,0:T(8,128)S(1)}, f32[5,2,20,128]{3,2,1,0:T(8,128)S(1)}, u32[]{:S(2)}, u32[]{:S(2)}) collective-permute-start(f32[5,2,20,128]{3,2,1,0:T(8,128)S(1)} %get-tuple-element.69), channel_id=1, source_target_pairs={{1,0},{2,1},{3,2},{5,4},{6,5},{7,6},{9,8},{10,9},{11,10},{13,12},{... | collective-permute-start | bytes 307208 | tf_op jit(solution)/shard_map/ppermute | solution.py:25
  74.1 9.1 %collective-permute-start.6 = (f32[5,2,20,128]{3,2,1,0:T(8,128)S(1)}, f32[5,2,20,128]{3,2,1,0:T(8,128)S(1)}, u32[]{:S(2)}, u32[]{:S(2)}) collective-permute-start(f32[5,2,20,128]{3,2,1,0:T(8,128)S(1)} %get-tuple-element.70), channel_id=1, source_target_pairs={{0,1},{1,2},{2,3},{4,5},{5,6},{6,7},{8,9},{9,10},{10,11},{12,13},{... | collective-permute-start | bytes 307208 | tf_op jit(solution)/shard_map/ppermute | solution.py:22
  79.5 3.6 %copy-start.3 = (f32[10,16,128]{2,1,0:T(8,128)S(1)}, f32[10,16,128]{2,1,0:T(8,128)}, u32[]{:S(2)}) copy-start(f32[10,16,128]{2,1,0:T(8,128)} %copy.54) | copy-start | bytes 245764
  84.2 7.7 %collective-permute-start.9 = (f32[5,8,2,128]{3,2,1,0:T(2,128)S(1)}, f32[5,8,2,128]{3,2,1,0:T(2,128)S(1)}, u32[]{:S(2)}, u32[]{:S(2)}) collective-permute-start(f32[5,8,2,128]{3,2,1,0:T(2,128)S(1)} %get-tuple-element.79), channel_id=1, source_target_pairs={{4,0},{8,4},{12,8},{16,12},{20,16},{24,20},{28,24},{32,28},{36,32}... | collective-permute-start | bytes 122888 | tf_op jit(solution)/shard_map/ppermute | solution.py:25
  87.9 6.2 %collective-permute-start.8 = (f32[5,8,2,128]{3,2,1,0:T(2,128)S(1)}, f32[5,8,2,128]{3,2,1,0:T(2,128)S(1)}, u32[]{:S(2)}, u32[]{:S(2)}) collective-permute-start(f32[5,8,2,128]{3,2,1,0:T(2,128)S(1)} %get-tuple-element.80), channel_id=1, source_target_pairs={{0,4},{4,8},{8,12},{12,16},{16,20},{20,24},{24,28},{28,32},{32,36}... | collective-permute-start | bytes 122888 | tf_op jit(solution)/shard_map/ppermute | solution.py:22
  94.3 9.5 %collective-permute-start.11 = (f32[5,2,20,128]{3,2,1,0:T(8,128)S(1)}, f32[5,2,20,128]{3,2,1,0:T(8,128)S(1)}, u32[]{:S(2)}, u32[]{:S(2)}) collective-permute-start(f32[5,2,20,128]{3,2,1,0:T(8,128)S(1)} %get-tuple-element.67), channel_id=1, source_target_pairs={{1,0},{2,1},{3,2},{5,4},{6,5},{7,6},{9,8},{10,9},{11,10},{13,12},{... | collective-permute-start | bytes 307208 | tf_op jit(solution)/shard_map/ppermute | solution.py:25
  95.6 8.3 %collective-permute-start.10 = (f32[5,2,20,128]{3,2,1,0:T(8,128)S(1)}, f32[5,2,20,128]{3,2,1,0:T(8,128)S(1)}, u32[]{:S(2)}, u32[]{:S(2)}) collective-permute-start(f32[5,2,20,128]{3,2,1,0:T(8,128)S(1)} %get-tuple-element.68), channel_id=1, source_target_pairs={{0,1},{1,2},{2,3},{4,5},{5,6},{6,7},{8,9},{9,10},{10,11},{12,13},{... | collective-permute-start | bytes 307208 | tf_op jit(solution)/shard_map/ppermute | solution.py:22
  104.3 69.9 %copy-start.5 = (f32[24,4,128]{2,1,0:T(4,128)S(1)}, f32[24,4,128]{2,1,0:T(4,128)}, u32[]{:S(2)}) copy-start(f32[24,4,128]{2,1,0:T(4,128)} %get-tuple-element.118) | copy-start | bytes 147460
  104.3 69.9 %copy-start.6 = (f32[24,4,128]{2,1,0:T(4,128)S(1)}, f32[24,4,128]{2,1,0:T(4,128)}, u32[]{:S(2)}) copy-start(f32[24,4,128]{2,1,0:T(4,128)} %get-tuple-element.123) | copy-start | bytes 147460
  104.3 69.9 %copy-start.7 = (f32[24,4,128]{2,1,0:T(4,128)S(1)}, f32[24,4,128]{2,1,0:T(4,128)}, u32[]{:S(2)}) copy-start(f32[24,4,128]{2,1,0:T(4,128)} %get-tuple-element.124) | copy-start | bytes 147460
  104.3 69.9 %copy-start.8 = (f32[24,4,128]{2,1,0:T(4,128)S(1)}, f32[24,4,128]{2,1,0:T(4,128)}, u32[]{:S(2)}) copy-start(f32[24,4,128]{2,1,0:T(4,128)} %get-tuple-element.127) | copy-start | bytes 147460
  104.3 69.9 %copy-start.9 = (f32[24,4,128]{2,1,0:T(4,128)S(1)}, f32[24,4,128]{2,1,0:T(4,128)}, u32[]{:S(2)}) copy-start(f32[24,4,128]{2,1,0:T(4,128)} %get-tuple-element.128) | copy-start | bytes 147460
  104.4 69.9 %copy-start.10 = (f32[24,4,128]{2,1,0:T(4,128)S(1)}, f32[24,4,128]{2,1,0:T(4,128)}, u32[]{:S(2)}) copy-start(f32[24,4,128]{2,1,0:T(4,128)} %get-tuple-element.129) | copy-start | bytes 147460
  104.4 69.9 %copy-start.11 = (f32[24,4,128]{2,1,0:T(4,128)S(1)}, f32[24,4,128]{2,1,0:T(4,128)}, u32[]{:S(2)}) copy-start(f32[24,4,128]{2,1,0:T(4,128)} %get-tuple-element.130) | copy-start | bytes 147460
  104.6 70.6 %copy-start.4 = (f32[5,8,16,128]{3,2,1,0:T(8,128)}, f32[5,8,16,128]{3,2,1,0:T(8,128)S(1)}, u32[]{:S(2)}) copy-start(f32[5,8,16,128]{3,2,1,0:T(8,128)S(1)} %fusion.89) | copy-start | bytes 983044
Sparse Core Ops, SparseCore 0:
  105.5 67.0 all-reduce.4
